TPU v7x, 256 devices: a whole 4x4x8 slice. The times are simulated.
256 devices in a mesh: prow: 16 (over x, y), pcol: 16 (over z, core).
Axes of the slice: x: 4, y: 4, z: 8, core: 2. Of those that a mesh axis runs over, the one named last changes fastest.
Arguments:
- inverse_tiles: float32 [24576, 24576], P('prow', 'pcol'), may hold values from -6 to 6
- factor_rows: float32 [24576, 512], P('prow'), may hold values from -0.0390625 to 0.0390625
- diag_inverse: float32 [512, 512], P('prow', 'pcol'), may hold values from -6 to 6
- pattern: int32 [192], replicated, may hold values from 0 to 1, as said below
Outputs:
- column_block: float32 [24576, 512], P(('prow', 'pcol'))
- diagonal_block: float32 [512, 512], P('prow', 'pcol')
Inputs may be any that keep to these rules, and one draw needn't show every extreme that they name: `pattern`: 1 where the block of ancestor rows lies in the supernode's structure, else 0; the first block always lies in it and the last never.
All inputs are finite; a program needn't handle non-finite values.
Results may differ from a plain program's by a relative error of at most 0.000078.
Values sent between devices are 32-bit elements; how exact they have to be, the bound alone decides.
A program may use at most 64 MiB of HBM per device.

v0:
```python
import jax
import jax.numpy as jnp
from jax import lax
from jax.sharding import PartitionSpec as P

BLK = 128


def broadcast(shard, axis, root):
    mine = lax.axis_index(axis) == root
    return lax.psum(jnp.where(mine, shard, jnp.zeros_like(shard)), axis)


def row_select(pattern, first_row, row_count):
    global_rows = first_row + lax.iota(jnp.int32, row_count)
    block_ids = global_rows // BLK
    blocks = lax.iota(jnp.int32, pattern.shape[0])
    match = block_ids[:, None] == blocks[None, :]
    return jnp.sum(jnp.where(match, pattern[None, :], 0), axis=1).astype(jnp.float32)


def local(inverse_tiles, factor_rows, diag_inverse, pattern):
    n_row = lax.axis_size("prow")
    n_col = lax.axis_size("pcol")
    row_index = lax.axis_index("prow")
    col_index = lax.axis_index("pcol")
    tile_rows = inverse_tiles.shape[0]
    width = factor_rows.shape[1]
    col_ratio = n_col // n_row
    tile_mask = row_select(pattern, row_index * tile_rows, tile_rows)
    masked_rows = factor_rows * tile_mask[:, None]
    root_index = col_index // col_ratio
    column_factor = broadcast(masked_rows, "prow", root_index)
    out_rows = tile_rows // n_col
    own_mask = lax.dynamic_slice_in_dim(tile_mask, col_index * out_rows, out_rows, 0)
    summed = lax.psum_scatter(
        jnp.dot(
            inverse_tiles,
            column_factor,
            precision=lax.Precision.HIGHEST,
            preferred_element_type=jnp.float32,
        ),
        "pcol",
        scatter_dimension=0,
        tiled=True,
    )
    column_block = -summed * own_mask[:, None]
    own_factor = lax.dynamic_slice_in_dim(masked_rows, col_index * out_rows, out_rows, 0)
    correction = jnp.dot(
        own_factor.T,
        column_block,
        precision=lax.Precision.HIGHEST,
        preferred_element_type=jnp.float32,
    )
    share_rows = width // n_row
    share_cols = width // n_col
    total = lax.psum(correction, ("prow", "pcol"))
    mine = lax.dynamic_slice_in_dim(total, row_index * share_rows, share_rows, 0)
    mine = lax.dynamic_slice_in_dim(mine, col_index * share_cols, share_cols, 1)
    diagonal_block = diag_inverse - mine
    return (column_block, diagonal_block)


def solution(mesh):
    return jax.shard_map(
        local,
        mesh=mesh,
        in_specs=(P("prow", "pcol"), P("prow", None), P("prow", "pcol"), P()),
        out_specs=(P(("prow", "pcol"), None), P("prow", "pcol")),
        check_vma=False,
    )
```

profile of v0, /device:TPU:1, one launch (start us, length us, event | category | flops | bytes accessed | tf_op | source)
XLA Modules:
  0.0 486.1 jit_solution(2618782349382456584)
XLA Ops:
  7.2 0.0 all-reduce.3.cloned.1.call-start
  7.2 0.9 select_reduce_fusion
  8.2 4.1 broadcast_select_fusion
  12.2 0.0 all-reduce.3.cloned.1.call-update
  12.3 0.0 reduce-scatter.4.cloned.1.call-start
  12.3 109.3 %all-reduce.3.cloned.1.call-done = f32[1536,512]{1,0:T(8,128)} async-done(((f32[1536,512]{1,0:T(8,128)}), f32[1536,512]{1,0:T(8,128)}) %all-reduce.3.cloned.1.call-update) | async-done | bytes 3145744 | tf_op jit(solution)/shard_map/psum | solution.py:11
  121.7 33.8 %convolution_bitcast_fusion = f32[1536,512]{0,1:T(8,128)} fusion(f32[1536,512]{1,0:T(8,128)} %all-reduce.3.cloned.1.call-done, f32[1536,1536]{1,0:T(8,128)} %param.4), kind=kOutput, calls=%fused_computation | convolution fusion | flops 14495514624 | bytes 15728640 | tf_op jit(solution)/shard_map/dot_general | solution.py:37
  155.4 3.5 copy.9
  159.0 0.0 copy-start
  159.0 0.0 reduce-scatter.4.cloned.1.call-update
  159.0 0.0 all-reduce.5.cloned.1.call-start
  159.1 0.1 dynamic_slice.10
  159.1 57.6 %reduce-scatter.4.cloned.1.call-done = f32[96,512]{1,0:T(8,128)} async-done(((f32[1536,512]{1,0:T(8,128)}), f32[96,512]{1,0:T(8,128)}) %reduce-scatter.4.cloned.1.call-update) | async-done | bytes 196624
  216.7 1.8 copy.10
  218.4 1.0 negate_multiply_fusion
  219.4 2.1 fusion
  221.5 0.0 all-reduce.5.cloned.1.call-update
  221.5 0.8 copy.8
  222.3 255.8 %all-reduce.5.cloned.1.call-done = f32[512,512]{1,0:T(8,128)} async-done(((f32[512,512]{1,0:T(8,128)}), f32[512,512]{1,0:T(8,128)}) %all-reduce.5.cloned.1.call-update) | async-done | bytes 1048592 | tf_op jit(solution)/shard_map/psum | solution.py:57
  478.1 0.0 copy-done
  478.1 1.5 dynamic-slice_subtract_fusion
  (2 shorter events, 0.0 us)
Async XLA Ops:
  7.2 114.5 %all-reduce.3.cloned.1.call-start = ((), (), s32[]{:S(2)}) async-start(), calls=%async_computation.1 | async-start | bytes 6291456 | tf_op jit(solution)/shard_map/psum | solution.py:11
  12.3 204.4 %reduce-scatter.4.cloned.1.call-start = ((), (), s32[]{:S(2)}) async-start(), calls=%async_computation.3 | async-start | bytes 3342336
  159.0 319.1 %copy-start = (f32[32,32]{1,0:T(8,128)S(1)}, f32[32,32]{1,0:T(8,128)}, u32[]{:S(2)}) copy-start(f32[32,32]{1,0:T(8,128)} %param.6) | copy-start | bytes 12292
  159.0 319.1 %all-reduce.5.cloned.1.call-start = ((), (), s32[]{:S(2)}) async-start(), calls=%async_computation.2 | async-start | bytes 2097152 | tf_op jit(solution)/shard_map/psum | solution.py:57
Sparse Core Ops, SparseCore 0:
  12.4 109.2 all-reduce.2
  159.1 57.5 reduce-scatter.3
  222.1 255.9 all-reduce.4
where the time goes:
time: 487 us; the launch traced here: 486 us
  waiting for transfers between devices  423 us (87%)
  matrix products  35.8 us (7%)
  between operations  13.8 us (3%)
  other arithmetic  7.43 us (2%)
  local copies, waits for them, and re-layouts  6.18 us (1%)
    psum x1, waiting for transfers between devices, local(): total = lax.psum(correction, ('prow', 'pcol'))  256 us
    psum x1, waiting for transfers between devices, broadcast(): return lax.psum(jnp.where(mine, shard, jnp.zeros_like(shard)), axis)  109 us
    unnamed x4, waiting for transfers between devices  57.6 us
    dot_general x1, matrix products, local(): jnp.dot(inverse_tiles, column_factor, precision=lax.Precision.HIGHEST, pr...  33.8 us
  transfers between devices with their start and end apart: 3, of which 3 were waited for; matrix products, arithmetic and copies ran while one was open for 0% of the time, Pallas kernels for 0%

commit v1 on v0

v1 whole, which is shorter than its diff:
```python
import jax
import jax.numpy as jnp
from jax import lax
from jax.experimental import pallas as pl
from jax.experimental.pallas import tpu as pltpu
from jax.sharding import PartitionSpec as P

MESH = pl.DeviceIdType.MESH
F32 = jnp.float32
BF16 = jnp.bfloat16

BLK = 128
NX, NY, NZ, NC = 4, 4, 8, 2
NR = NX * NY
NP = NZ * NC
TILE = 1536
SH = TILE // NP
HP = SH // 2
W = 512
WC = 128
NCH = W // WC
DR = W // NR


def split(v):
    hi = v.astype(BF16)
    lo = (v - hi.astype(F32)).astype(BF16)
    return hi, lo


def kernel(
    pat, a_hbm, f_hbm, col_ref, d_ref,
    a32, ahi, alo, fown, fc, fs, pb, xb, zb, dp, db, dz, fthi, ftlo, qs,
    a_sem, f_sem, sc_s, sc_r, own_s, b_s, b_r, c_s, c_r, x_s, x_r, z_s, z_r, d_s, d_r, e_s, e_r,
):
    r = lax.axis_index("prow")
    c = lax.axis_index("pcol")
    x, y = r // NY, r % NY
    z, core = c // NC, c % NC
    is_root = r == c

    def share_of(s):
        h, zz = s // NZ, s % NZ
        dest_core = jnp.where(h == 0, 1 - core, core)
        return NC * zz + dest_core

    def slot_of(share):
        return jnp.where(share % NC == core, NZ, 0) + share // NC

    def f_load(s):
        return pltpu.make_async_copy(f_hbm.at[share_of(s)], fown.at[s], f_sem.at[s])

    def a_load(s):
        return pltpu.make_async_copy(a_hbm.at[share_of(s)], a32.at[s], a_sem.at[s])

    @pl.loop(0, NP)
    def _(s):
        f_load(s).start()

    @pl.loop(0, NP)
    def _(s):
        a_load(s).start()

    barrier = pltpu.get_barrier_semaphore()

    @pl.loop(1, NR)
    def _(k):
        pl.semaphore_signal(barrier, inc=1, device_id=((r + k) % NR, c), device_id_type=MESH)

    @pl.loop(1, NZ)
    def _(k):
        pl.semaphore_signal(barrier, inc=1, device_id=(r, (c + NC * k) % NP), device_id_type=MESH)

    @pl.loop(0, NZ)
    def _(k):
        pl.semaphore_signal(barrier, inc=1, device_id=(r, (NC * ((z + k) % NZ) + 1 - core)), device_id_type=MESH)

    pl.semaphore_wait(barrier, NR - 1 + NZ - 1 + NZ)

    @pl.loop(0, NP)
    def _(s):
        f_load(s).wait()

    def cols(j):
        return pl.ds(j * WC, WC)

    def scatter(j):
        @pl.when(is_root)
        def _():
            @pl.loop(1, NR)
            def _(k):
                to = (r + k) % NR
                pltpu.make_async_remote_copy(
                    src_ref=fown.at[slot_of(to), :, :, cols(j)],
                    dst_ref=fc.at[j, to // NY, to % NY],
                    send_sem=sc_s.at[j], recv_sem=sc_r.at[j],
                    device_id=(to, c), device_id_type=MESH,
                ).start()
            pltpu.make_async_copy(fown.at[slot_of(r), :, :, cols(j)], fc.at[j, x, y], own_s.at[j]).start()

    def scatter_recv(j):
        @pl.when(is_root)
        def _():
            pltpu.make_async_copy(fown.at[slot_of(r), :, :, cols(j)], fc.at[j, x, y], own_s.at[j]).wait()

        @pl.when(jnp.logical_not(is_root))
        def _():
            pltpu.make_async_copy(fc.at[j, x, y], fc.at[j, x, y], sc_r.at[j]).wait()

    def scatter_sent(j):
        @pl.when(is_root)
        def _():
            part = fown.at[pl.ds(0, NR - 1), :, :, cols(j)]
            pltpu.make_async_copy(part, part, sc_s.at[j]).wait()

    def xpeer(k):
        return (((x + k) % NX) * NY + y, c)

    def ypeer(k):
        return (x * NY + (y + k) % NY, c)

    def ring_copies(j, stage):
        ssem, rsem = (b_s, b_r) if stage == 0 else (c_s, c_r)
        out = []
        for k in range(1, 4):
            for h in range(2):
                if stage == 0:
                    mine = fc.at[j, x, y, h]
                elif h == 0:
                    mine = fc.at[j, x, :, 0]
                else:
                    mine = fc.at[j, :, y, 1]
                peer = ypeer(k) if (stage == 0) == (h == 0) else xpeer(k)
                out.append(pltpu.make_async_remote_copy(
                    src_ref=mine, dst_ref=mine, send_sem=ssem.at[j, h, k - 1], recv_sem=rsem.at[j, h, k - 1],
                    device_id=peer, device_id_type=MESH))
        return out

    def ring_send(j, stage):
        for copy in ring_copies(j, stage):
            copy.start()

    def ring_recv(j, stage):
        for copy in ring_copies(j, stage):
            copy.wait_recv()

    def ring_sent(j, stage):
        for copy in ring_copies(j, stage):
            copy.wait_send()

    def split_a(first, last):
        @pl.loop(first, last)
        def _(s):
            a_load(s).wait()

            @pl.loop(0, SH // 16)
            def _(t):
                hi, lo = split(a32[s, pl.ds(pl.multiple_of(t * 16, 16), 16), :])
                rows = pl.ds(pl.multiple_of(s * SH + t * 16, 16), 16)
                ahi[rows, :] = hi
                alo[rows, :] = lo

    def transpose_f():
        for g in range(2):
            masks = []
            for q in range(12):
                row = r * TILE + SH * (NC * (4 * g + q // 3) + core) + 32 * (q % 3)
                masks.append(pat[row // BLK].astype(F32))
            for cb in range(W // 128):
                v = fown[pl.ds(NZ + 4 * g, 4), :, :, pl.ds(cb * 128, 128)].reshape(4 * SH, 128)
                for b in range(3):
                    part = jnp.concatenate(
                        [v[128 * b + 32 * q: 128 * b + 32 * q + 32] * masks[4 * b + q] for q in range(4)], axis=0)
                    hi, lo = split(part.T)
                    at = (pl.ds(cb * 128, 128), pl.ds((3 * g + b) * 128, 128))
                    fthi[at] = hi
                    ftlo[at] = lo

    def split_f(j):
        for xx in range(NX):
            v = fc[j, xx].reshape(NY * SH, WC)
            for b in range(3):
                hi, lo = split(v[b * BLK:(b + 1) * BLK] * pat[c * (TILE // BLK) + 3 * xx + b].astype(F32))
                rows = pl.ds((3 * xx + b) * BLK, BLK)
                fs[rows, 0:WC] = hi
                fs[rows, WC:2 * WC] = lo

    def product(j, h):
        @pl.loop(0, 2)
        def _(t):
            rows = pl.ds(pl.multiple_of(h * NZ * SH + t * 4 * SH, 4 * SH), 4 * SH)
            p = jnp.dot(ahi[rows, :], fs[...], preferred_element_type=F32)
            q = jnp.dot(alo[rows, :], fs[:, 0:WC], preferred_element_type=F32)
            pb[j, h, pl.ds(t * 4, 4)] = (p[:, 0:WC] + (p[:, WC:2 * WC] + q)).reshape(4, SH, WC)

    def exchange(j):
        return pltpu.make_async_remote_copy(
            src_ref=pb.at[j, 0], dst_ref=xb.at[j], send_sem=x_s.at[j], recv_sem=x_r.at[j],
            device_id=(r, c + 1 - 2 * core), device_id_type=MESH)

    def add_exchanged(j):
        exchange(j).wait_recv()
        @pl.loop(0, NZ)
        def _(zz):
            v = pb[j, 1, zz] + xb[j, zz]
            pb[j, 1, zz] = v

    def z_send(j):
        @pl.loop(1, NZ)
        def _(k):
            to = (z + k) % NZ
            pltpu.make_async_remote_copy(
                src_ref=pb.at[j, 1, to], dst_ref=zb.at[j, k - 1], send_sem=z_s.at[j], recv_sem=z_r.at[j],
                device_id=(r, NC * to + core), device_id_type=MESH).start()

    def z_finish(j):
        pltpu.make_async_copy(zb.at[j], zb.at[j], z_r.at[j]).wait()
        total = pb[j, 1, z]
        for k in range(NZ - 1):
            total += zb[j, k]
        for q in range(3):
            row = r * TILE + SH * c + 32 * q
            col_ref[pl.ds(32 * q, 32), cols(j)] = total[32 * q:32 * q + 32] * pat[row // BLK].astype(F32)

    def z_sent(j):
        part = pb.at[j, 1, pl.ds(0, NZ - 1)]
        pltpu.make_async_copy(part, part, z_s.at[j]).wait()

    def diag_product(j):
        for g in range(2):
            v = pb[j, 1, pl.ds(4 * g, 4)].reshape(4 * SH, WC)
            hi, lo = split(v)
            qs[pl.ds(g * 4 * SH, 4 * SH), 0:WC] = hi
            qs[pl.ds(g * 4 * SH, 4 * SH), WC:2 * WC] = lo
        p = jnp.dot(fthi[...], qs[...], preferred_element_type=F32)
        q = jnp.dot(ftlo[...], qs[:, 0:WC], preferred_element_type=F32)
        dp[j] = (p[:, 0:WC] + (p[:, WC:2 * WC] + q)).reshape(NR, DR, WC)

    def d_send(j):
        @pl.loop(1, NR)
        def _(k):
            to = (r + k) % NR
            pltpu.make_async_remote_copy(
                src_ref=dp.at[j, to], dst_ref=db.at[j, k - 1], send_sem=d_s.at[j], recv_sem=d_r.at[j],
                device_id=(to, c), device_id_type=MESH).start()

    def d_sent(j):
        part = dp.at[j, pl.ds(0, NR - 1)]
        pltpu.make_async_copy(part, part, d_s.at[j]).wait()

    def e_copy(j, dest):
        return pltpu.make_async_remote_copy(
            src_ref=db.at[j, NR - 1], dst_ref=dz.at[c], send_sem=e_s.at[j, dest], recv_sem=e_r.at[c],
            device_id=(r, 4 * j + dest), device_id_type=MESH)

    def d_finish(j):
        pltpu.make_async_copy(db.at[j, pl.ds(0, NR - 1)], db.at[j, pl.ds(0, NR - 1)], d_r.at[j]).wait()
        total = dp[j, r]
        for k in range(NR - 1):
            total += db[j, k]
        db[j, NR - 1] = total
        for dest in range(4):
            @pl.when(c != 4 * j + dest)
            def _():
                e_copy(j, dest).start()

        @pl.when(c // 4 == j)
        def _():
            dz[c] = total

    def e_sent(j):
        for dest in range(4):
            @pl.when(c != 4 * j + dest)
            def _():
                e_copy(j, dest).wait_send()

    for j in range(NCH):
        scatter(j)

    def relay(step):
        if 0 <= step - 1 < NCH:
            ring_recv(step - 1, 0)
            ring_send(step - 1, 1)
        if step < NCH:
            scatter_recv(step)
            ring_send(step, 0)

    def compute(j):
        ring_recv(j, 1)
        split_f(j)
        product(j, 0)
        exchange(j).start()
        product(j, 1)

    def reduce(j):
        add_exchanged(j)
        z_send(j)
        diag_product(j)
        d_send(j)

    def finish(j):
        d_finish(j)
        z_finish(j)

    split_a(0, 4)
    relay(0)
    split_a(4, 10)
    relay(1)
    split_a(10, 16)
    transpose_f()
    relay(2)
    for j in range(NCH):
        compute(j)
        relay(j + 3)
        reduce(j)
        if j >= 1:
            finish(j - 1)
    for j in range(NCH):
        scatter_sent(j)
        ring_sent(j, 0)
        ring_sent(j, 1)
        exchange(j).wait_send()
    finish(NCH - 1)
    for j in range(NCH):
        z_sent(j)
        d_sent(j)
        e_sent(j)

    for k in range(1, NP):
        src = (c + k) % NP
        pltpu.make_async_copy(dz.at[src], dz.at[src], e_r.at[src]).wait()
    total = dz[0]
    for k in range(1, NP):
        total += dz[k]
    d_ref[...] = total


def local(inverse_tiles, factor_rows, diag_inverse, pattern):
    c = lax.axis_index("pcol")
    dma = pltpu.SemaphoreType.DMA
    col, d = pl.pallas_call(
        kernel,
        out_shape=(jax.ShapeDtypeStruct((SH, W), F32), jax.ShapeDtypeStruct((DR, WC), F32)),
        in_specs=[
            pl.BlockSpec(memory_space=pltpu.SMEM),
            pl.BlockSpec(memory_space=pl.ANY),
            pl.BlockSpec(memory_space=pl.ANY),
        ],
        out_specs=(pl.BlockSpec(memory_space=pltpu.VMEM), pl.BlockSpec(memory_space=pltpu.VMEM)),
        scratch_shapes=[
            pltpu.VMEM((NP, SH, TILE), F32),
            pltpu.VMEM((TILE, TILE), BF16),
            pltpu.VMEM((TILE, TILE), BF16),
            pltpu.VMEM((NP, 2, HP, W), F32),
            pltpu.VMEM((NCH, NX, NY, 2, HP, WC), F32),
            pltpu.VMEM((TILE, 2 * WC), BF16),
            pltpu.VMEM((NCH, 2, NZ, SH, WC), F32),
            pltpu.VMEM((NCH, NZ, SH, WC), F32),
            pltpu.VMEM((NCH, NZ - 1, SH, WC), F32),
            pltpu.VMEM((NCH, NR, DR, WC), F32),
            pltpu.VMEM((NCH, NR, DR, WC), F32),
            pltpu.VMEM((NP, DR, WC), F32),
            pltpu.VMEM((W, NZ * SH), BF16),
            pltpu.VMEM((W, NZ * SH), BF16),
            pltpu.VMEM((NZ * SH, 2 * WC), BF16),
            dma((NP,)), dma((NP,)),
            dma((NCH,)), dma((NCH,)), dma((NCH,)),
            dma((NCH, 2, 3)), dma((NCH, 2, 3)),
            dma((NCH, 2, 3)), dma((NCH, 2, 3)),
            dma((NCH,)), dma((NCH,)),
            dma((NCH,)), dma((NCH,)),
            dma((NCH,)), dma((NCH,)),
            dma((NCH, 4)), dma((NP,)),
        ],
        compiler_params=pltpu.CompilerParams(collective_id=1, has_side_effects=True, vmem_limit_bytes=60 << 20),
        name="selected_inversion",
    )(pattern, inverse_tiles.reshape(NP, SH, TILE), factor_rows.reshape(NP, 2, HP, W))
    mine = lax.dynamic_slice_in_dim(d, (c % 4) * DR, DR, 1)
    return -col, diag_inverse + mine


def solution(mesh):
    return jax.shard_map(
        local,
        mesh=mesh,
        in_specs=(P("prow", "pcol"), P("prow", None), P("prow", "pcol"), P()),
        out_specs=(P(("prow", "pcol"), None), P("prow", "pcol")),
        check_vma=False,
    )
```

time: 487 us -> 97.3 us (0.20)
  waiting for transfers between devices: 423 us -> 0 us
  Pallas kernels: 0 us -> 93.4 us
  matrix products: 35.8 us -> 0 us
  between operations: 13.8 us -> 0.67 us
  local copies, waits for them, and re-layouts: 6.18 us -> 0.01 us
    psum x2 -> x0, waiting for transfers between devices: 365 us -> none  [the longest x1 256 us: local(): total = lax.psum(correction, ('prow', 'pcol'))]
    pallas_call x0 -> x1, Pallas kernels: none -> 93.4 us  [local(): pl.pallas_call(kernel, out_shape=(jax.ShapeDtypeStruct((SH, W), F32), jax...]
    unnamed x4 -> x0, waiting for transfers between devices: 57.6 us -> none
    dot_general x2 -> x0, matrix products: 35.8 us -> none  [the longest x1 33.8 us: local(): jnp.dot(inverse_tiles, column_factor, precision=lax.Precision.HIGHEST, pr...]
    unnamed x5 -> x2, local copies, waits for them, and re-layouts: 6.1 us -> 0.01 us
  transfers between devices with their start and end apart: 3 -> 0, of which waited for: 3 -> 0; matrix products, arithmetic and copies ran while one was open for 0% -> 0% of each run, Pallas kernels for 0% -> 0%
where the time goes in v1:
time: 97.3 us; the launch traced here: 97.1 us
  Pallas kernels  93.4 us (96%)
  other arithmetic  3.02 us (3%)
    pallas_call x1, Pallas kernels, local(): pl.pallas_call(kernel, out_shape=(jax.ShapeDtypeStruct((SH, W), F32), jax...  93.4 us

profile of v1, /device:TPU:1, one launch (start us, length us, event | category | flops | bytes accessed | tf_op | source)
XLA Modules:
  0.0 97.1 jit_solution(10566906565774875501)
XLA Ops:
  0.6 0.0 copy-start
  0.7 93.4 %selected_inversion.1 = (f32[96,512]{1,0:T(8,128)}, f32[32,128]{1,0:T(8,128)}) custom-call(s32[192]{0:T(256)} %pat.1, f32[16,96,1536]{2,1,0:T(8,128)} %bitcast.2, f32[16,2,48,512]{3,2,1,0:T(8,128)} %bitcast.3), custom_call_target="tpu_custom_call" | custom-call | tf_op jit(solution)/shard_map/selected_inversion/pallas_call | solution.py:341
  94.1 0.0 copy-done
  94.1 1.4 %dynamic-slice_add_fusion = f32[32,32]{1,0:T(8,128)} fusion(f32[32,32]{1,0:T(8,128)S(1)} %copy-done, f32[32,128]{1,0:T(8,128)} %get-tuple-element.5, s32[]{:T(128)S(6)} %select_n.11), kind=kLoop, calls=%fused_computation | loop fusion | flops 1024 | bytes 12292 | tf_op jit(solution)/shard_map/add | solution.py:379
  95.5 1.6 %neg.3 = f32[96,512]{1,0:T(8,128)} negate(f32[96,512]{1,0:T(8,128)} %get-tuple-element.4) | non-fusion elementwise | flops 49152 | bytes 393216 | tf_op jit(solution)/shard_map/neg | solution.py:379
Async XLA Ops:
  0.6 93.4 %copy-start = (f32[32,32]{1,0:T(8,128)S(1)}, f32[32,32]{1,0:T(8,128)}, u32[]{:S(2)}) copy-start(f32[32,32]{1,0:T(8,128)} %param.6) | copy-start | bytes 12292

commit v2 on v0

v2 whole, which is shorter than its diff:
```python
import jax
import jax.numpy as jnp
from jax import lax
from jax.experimental import pallas as pl
from jax.experimental.pallas import tpu as pltpu
from jax.sharding import PartitionSpec as P

MESH = pl.DeviceIdType.MESH
F32 = jnp.float32
BF16 = jnp.bfloat16

BLK = 128
NX, NY, NZ, NC = 4, 4, 8, 2
NR = NX * NY
NP = NZ * NC
TILE = 1536
SH = TILE // NP
HP = SH // 2
W = 512
WC = 128
NCH = W // WC
DR = W // NR


DIRS = ((1, 0), (3, 0), (0, 1), (0, 3))
SEND = ((57344, 24321, 12544, 4352), (4017, 224, 560, 16), (8, 32776, 34944, 52429), (70, 8198, 17479, 8736))
DEPTH = ((23130, 60186, 1252), (23130, 7146, 58372), (23130, 55510, 10016), (23130, 29308, 36224))
QR = TILE // 4
NSUB = 2
SR = QR // NSUB
NS = NCH * NSUB
HOP = 3
PRE = 7
GROUPS = ((0, 1, 2), (3,))
ZCOPIES = (
    (-1, -3, 0, SH), (-2, -4, 0, HP), (1, 3, 0, SH), (2, 4, HP, HP),
    (-1, -1, 0, SH), (1, 1, 0, SH), (-2, -2, 0, SH), (2, 2, 0, SH),
)
XYORDER = ((2, 2), (1, 0), (3, 0), (0, 1), (0, 3), (1, 1), (3, 3), (1, 3), (3, 1), (2, 0), (0, 2), (2, 1), (1, 2), (2, 3), (3, 2))


def split(v):
    hi = v.astype(BF16)
    lo = (v - hi.astype(F32)).astype(BF16)
    return hi, lo


def kernel(
    pat, a_hbm, f_hbm, col_ref, d_ref,
    a32, ahi, alo, fown, fc, fs, pb, xb, zb, dp, db, dz, fthi, ftlo, qs,
    a_sem, f_sem, own_s, t_s, t_r, x_s, x_r, z_s, z_r, d_s, d_r, e_s, e_r,
):
    r = lax.axis_index("prow")
    c = lax.axis_index("pcol")
    x, y = r // NY, r % NY
    z, core = c // NC, c % NC
    is_root = r == c

    def share_of(s):
        h, zz = s // NZ, s % NZ
        dest_core = jnp.where(h == 0, 1 - core, core)
        return NC * zz + dest_core

    def f_load(s):
        return pltpu.make_async_copy(f_hbm.at[pl.ds(pl.multiple_of((NC * s + core) * SH, 8), SH)], fown.at[s], f_sem.at[s])

    def a_load(s):
        return pltpu.make_async_copy(a_hbm.at[share_of(s)], a32.at[s], a_sem.at[s])

    def root_load(j):
        return pltpu.make_async_copy(f_hbm.at[:, cols(j)], fc.at[j], own_s.at[j])

    def cols(j):
        return pl.ds(j * WC, WC)

    @pl.when(is_root)
    def _():
        for j in range(NCH):
            root_load(j).start()

    @pl.loop(0, NP)
    def _(s):
        a_load(s).start()

    for zz in range(NZ):
        f_load(zz).start()

    barrier = pltpu.get_barrier_semaphore()
    for dx, dy in XYORDER:
        pl.semaphore_signal(
            barrier, inc=1, device_id=((x + dx) % NX * NY + (y + dy) % NY, c), device_id_type=MESH)

    @pl.loop(1, NP)
    def _(k):
        pl.semaphore_signal(barrier, inc=1, device_id=(r, (c + k) % NP), device_id_type=MESH)

    root_x, root_y = c // NY, c % NY
    pos = (x - root_x + NX) % NX * NY + (y - root_y + NY) % NY
    depth = [sum(((DEPTH[t][k] >> pos) & 1) << k for k in range(3)) for t in range(4)]
    sends = [[(SEND[t][d] >> pos) & 1 for d in range(4)] for t in range(4)]
    rank = [sum((((depth[u] < depth[t]) | ((depth[u] == depth[t]) & (u < t))).astype(jnp.int32) for u in range(4) if u != t), 0) for t in range(4)]
    order = [sum(t * (rank[t] == k).astype(jnp.int32) for t in range(4)) for k in range(4)]
    peers = [((x + dx) % NX * NY + (y + dy) % NY, c) for dx, dy in DIRS]

    def piece(t, s):
        return fc.at[s // NSUB, pl.ds(pl.multiple_of(t * QR + (s % NSUB) * SR, 8), SR)]

    def tree_copy(t, s, d):
        return pltpu.make_async_remote_copy(
            src_ref=piece(t, s), dst_ref=piece(t, s), send_sem=t_s.at[t, d], recv_sem=t_r.at[t, s],
            device_id=peers[d], device_id_type=MESH)

    def tree_send(t, s):
        for d in range(4):
            @pl.when(sends[t][d] == 1)
            def _():
                tree_copy(t, s, d).start()

    def relay(n):
        for t in range(4):
            s = jnp.where(is_root, n, n - HOP * (depth[t] - 1))

            @pl.when((s >= 0) & (s < NS))
            def _():
                @pl.when(jnp.logical_not(is_root))
                def _():
                    pltpu.make_async_copy(piece(t, s), piece(t, s), t_r.at[t, s]).wait()
                tree_send(t, s)

    def tree_sent():
        for t in range(4):
            part = fc.at[:, pl.ds(t * QR, QR)]
            for d in range(4):
                @pl.when(sends[t][d] == 1)
                def _():
                    pltpu.make_async_copy(part, part, t_s.at[t, d]).wait()

    def split_a(first, last):
        @pl.loop(first, last)
        def _(s):
            for k in range(4):
                hi, lo = split(a32[s, :, pl.ds(pl.multiple_of(order[k] * QR, 128), QR)])
                at = (pl.ds(pl.multiple_of(s * SH, 16), SH), pl.ds(k * QR, QR))
                ahi[at] = hi
                alo[at] = lo

    def a_wait(first, last):
        @pl.loop(first, last)
        def _(s):
            a_load(s).wait()

    def transpose_f():
        for g in range(2):
            masks = []
            for q in range(12):
                row = r * TILE + SH * (NC * (4 * g + q // 3) + core) + 32 * (q % 3)
                masks.append(pat[row // BLK].astype(F32))
            for cb in range(W // 128):
                v = fown[pl.ds(4 * g, 4), :, pl.ds(cb * 128, 128)].reshape(4 * SH, 128)
                for b in range(3):
                    part = jnp.concatenate(
                        [v[128 * b + 32 * q: 128 * b + 32 * q + 32] * masks[4 * b + q] for q in range(4)], axis=0)
                    hi, lo = split(part.T)
                    at = (pl.ds(cb * 128, 128), pl.ds((3 * g + b) * 128, 128))
                    fthi[at] = hi
                    ftlo[at] = lo

    def split_f(j, pair):
        for k in (2 * pair, 2 * pair + 1):
            for b in range(QR // BLK):
                rows = pl.ds(pl.multiple_of(order[k] * QR + b * BLK, BLK), BLK)
                hi, lo = split(fc[j, rows] * pat[c * (TILE // BLK) + order[k] * (QR // BLK) + b].astype(F32))
                rows = pl.ds(k * QR + b * BLK, BLK)
                fs[rows, 0:WC] = hi
                fs[rows, WC:2 * WC] = lo

    def product(j, h, pair):
        rows, depths = pl.ds(h * NZ * SH, NZ * SH), pl.ds(pair * 2 * QR, 2 * QR)
        p = jnp.dot(ahi[rows, depths], fs[depths, :], preferred_element_type=F32)
        q = jnp.dot(alo[rows, depths], fs[depths, 0:WC], preferred_element_type=F32)
        v = (p[:, 0:WC] + (p[:, WC:2 * WC] + q)).reshape(NZ, SH, WC)
        pb[j, h] = v if pair == 0 else pb[j, h] + v

    def exchange(j):
        return pltpu.make_async_remote_copy(
            src_ref=pb.at[j, 0], dst_ref=xb.at[j], send_sem=x_s.at[j], recv_sem=x_r.at[j],
            device_id=(r, c + 1 - 2 * core), device_id_type=MESH)

    def ex_send(j):
        exchange(j).start()

    def ex_recv(j):
        exchange(j).wait_recv()

    def ex_sent(j):
        exchange(j).wait_send()

    def add_exchanged(j):
        @pl.loop(0, NZ)
        def _(zz):
            v = pb[j, 1, zz] + xb[j, zz]
            pb[j, 1, zz] = v

    def z_copy(j, slot):
        away, off, first, count = ZCOPIES[slot]
        rows = pl.ds(first, count)
        return pltpu.make_async_remote_copy(
            src_ref=pb.at[j, 1, (z + off + NZ) % NZ, rows], dst_ref=zb.at[j, slot, rows],
            send_sem=z_s.at[j], recv_sem=z_r.at[j, slot // 4],
            device_id=(r, (c + NC * away + NP) % NP), device_id_type=MESH)

    def z_send(j, slot):
        z_copy(j, slot).start()

    def z_recv(j, stage):
        part = zb.at[j, pl.ds(4 * stage, 3 + stage)]
        pltpu.make_async_copy(part, part, z_r.at[j, stage]).wait()

    def z_sent(j):
        part = zb.at[j, pl.ds(0, 7)]
        pltpu.make_async_copy(part, part, z_s.at[j]).wait()

    def z_add(j):
        for slot in range(4):
            _, _, first, count = ZCOPIES[slot]
            share, rows = (z + (NZ - 2 if slot < 2 else 2)) % NZ, pl.ds(first, count)
            pb[j, 1, share, rows] = pb[j, 1, share, rows] + zb[j, slot, rows]

    def z_first(j):
        for slot in (1, 3, 0, 2, 4, 5):
            z_send(j, slot)

    def z_second(j):
        z_recv(j, 0)
        z_add(j)
        for slot in (6, 7):
            z_send(j, slot)

    def z_finish(j):
        z_recv(j, 1)
        total = pb[j, 1, z] + ((zb[j, 4] + zb[j, 5]) + (zb[j, 6] + zb[j, 7]))
        for q in range(3):
            row = r * TILE + SH * c + 32 * q
            col_ref[pl.ds(32 * q, 32), cols(j)] = total[32 * q:32 * q + 32] * pat[row // BLK].astype(F32)

    def diag_product(j):
        for g in range(2):
            v = pb[j, 1, pl.ds(4 * g, 4)].reshape(4 * SH, WC)
            hi, lo = split(v)
            qs[pl.ds(g * 4 * SH, 4 * SH), 0:WC] = hi
            qs[pl.ds(g * 4 * SH, 4 * SH), WC:2 * WC] = lo
        p = jnp.dot(fthi[...], qs[...], preferred_element_type=F32)
        q = jnp.dot(ftlo[...], qs[:, 0:WC], preferred_element_type=F32)
        dp[:, :, cols(j)] = (p[:, 0:WC] + (p[:, WC:2 * WC] + q)).reshape(NR, DR, WC)

    def d_cols(g):
        return pl.ds(GROUPS[g][0] * WC, len(GROUPS[g]) * WC)

    def d_send(g):
        for k, (dx, dy) in enumerate(XYORDER, 1):
            to = (x + dx) % NX * NY + (y + dy) % NY
            pltpu.make_async_remote_copy(
                src_ref=dp.at[to, :, d_cols(g)], dst_ref=db.at[k - 1, :, d_cols(g)],
                send_sem=d_s.at[g], recv_sem=d_r.at[g],
                device_id=(to, c), device_id_type=MESH).start()

    def d_sent(g):
        part = dp.at[pl.ds(0, NR - 1), :, d_cols(g)]
        pltpu.make_async_copy(part, part, d_s.at[g]).wait()

    def e_copy(j, dest):
        return pltpu.make_async_remote_copy(
            src_ref=db.at[NR - 1, :, cols(j)], dst_ref=dz.at[c], send_sem=e_s.at[j], recv_sem=e_r.at[0],
            device_id=(r, 4 * j + dest), device_id_type=MESH)

    def d_recv(g):
        part = db.at[pl.ds(0, NR - 1), :, d_cols(g)]
        pltpu.make_async_copy(part, part, d_r.at[g]).wait()

    def e_send(j):
        for dest in range(4):
            @pl.when(c != 4 * j + dest)
            def _():
                e_copy(j, dest).start()

    def d_finish(g):
        d_recv(g)
        total = dp[r, :, d_cols(g)]
        for k in range(NR - 1):
            total += db[k, :, d_cols(g)]
        db[NR - 1, :, d_cols(g)] = total
        for i, j in enumerate(GROUPS[g]):
            e_send(j)

            @pl.when(c // 4 == j)
            def _():
                dz[c] = total[:, i * WC:(i + 1) * WC]

    def e_sent(j):
        pltpu.make_async_copy(dz.at[pl.ds(0, 3)], dz.at[pl.ds(0, 3)], e_s.at[j]).wait()

        @pl.when(c // 4 != j)
        def _():
            pltpu.make_async_copy(dz.at[0], dz.at[0], e_s.at[j]).wait()

    def e_recv():
        part = dz.at[pl.ds(0, NP - 1)]
        pltpu.make_async_copy(part, part, e_r.at[0]).wait()

    def early(j):
        split_f(j, 0)
        product(j, 0, 0)
        product(j, 1, 0)

    def late(j):
        split_f(j, 1)
        product(j, 0, 1)
        ex_send(j)
        product(j, 1, 1)

    def exchanged(j):
        ex_recv(j)
        add_exchanged(j)
        z_first(j)

    a_wait(0, PRE)
    split_a(0, PRE)
    pl.semaphore_wait(barrier, NR - 1 + NP - 1)

    @pl.when(is_root)
    def _():
        for j in range(NCH):
            root_load(j).wait()

    @pl.loop(0, 10)
    def _(n):
        relay(n)

        @pl.when(n < NP - PRE)
        def _():
            a_wait(n + PRE, n + PRE + 1)
            split_a(n + PRE, n + PRE + 1)

        @pl.when(n == NP - PRE)
        def _():
            for zz in range(NZ):
                f_load(zz).wait()
            transpose_f()

    relay(10)
    early(0)
    relay(11)
    relay(12)
    early(1)
    relay(13)
    late(0)
    relay(14)
    early(2)
    exchanged(0)
    relay(15)
    late(1)
    relay(16)
    early(3)
    exchanged(1)
    relay(17)
    late(2)
    diag_product(0)
    relay(18)
    exchanged(2)
    z_second(0)
    diag_product(1)
    z_second(1)
    diag_product(2)
    d_send(0)
    relay(19)
    late(3)
    exchanged(3)
    diag_product(3)
    d_send(1)
    z_second(2)
    z_second(3)
    tree_sent()
    d_finish(0)
    z_finish(0)
    d_finish(1)
    z_finish(1)
    z_finish(2)
    for j in range(NCH):
        ex_sent(j)
        z_sent(j)
    z_finish(3)
    for j in range(NCH):
        e_sent(j)
    for g in range(2):
        d_sent(g)
    e_recv()
    total = dz[0]
    for k in range(1, NP):
        total += dz[k]
    d_ref[...] = total


def local(inverse_tiles, factor_rows, diag_inverse, pattern):
    c = lax.axis_index("pcol")
    dma = pltpu.SemaphoreType.DMA
    col, d = pl.pallas_call(
        kernel,
        out_shape=(jax.ShapeDtypeStruct((SH, W), F32), jax.ShapeDtypeStruct((DR, WC), F32)),
        in_specs=[
            pl.BlockSpec(memory_space=pltpu.SMEM),
            pl.BlockSpec(memory_space=pl.ANY),
            pl.BlockSpec(memory_space=pl.ANY),
        ],
        out_specs=(pl.BlockSpec(memory_space=pltpu.VMEM), pl.BlockSpec(memory_space=pltpu.VMEM)),
        scratch_shapes=[
            pltpu.VMEM((NP, SH, TILE), F32),
            pltpu.VMEM((TILE, TILE), BF16),
            pltpu.VMEM((TILE, TILE), BF16),
            pltpu.VMEM((NZ, SH, W), F32),
            pltpu.VMEM((NCH, TILE, WC), F32),
            pltpu.VMEM((TILE, 2 * WC), BF16),
            pltpu.VMEM((NCH, 2, NZ, SH, WC), F32),
            pltpu.VMEM((NCH, NZ, SH, WC), F32),
            pltpu.VMEM((NCH, 8, SH, WC), F32),
            pltpu.VMEM((NR, DR, W), F32),
            pltpu.VMEM((NR, DR, W), F32),
            pltpu.VMEM((NP, DR, WC), F32),
            pltpu.VMEM((W, NZ * SH), BF16),
            pltpu.VMEM((W, NZ * SH), BF16),
            pltpu.VMEM((NZ * SH, 2 * WC), BF16),
            dma((NP,)), dma((NZ,)),
            dma((NCH,)), dma((4, 4)), dma((4, NS)),
            dma((NCH,)), dma((NCH,)),
            dma((NCH,)), dma((NCH, 2)),
            dma((2,)), dma((2,)),
            dma((NCH,)), dma((1,)),
        ],
        compiler_params=pltpu.CompilerParams(collective_id=1, has_side_effects=True, vmem_limit_bytes=60 << 20),
        name="selected_inversion",
    )(pattern, inverse_tiles.reshape(NP, SH, TILE), factor_rows)
    mine = lax.dynamic_slice_in_dim(d, (c % 4) * DR, DR, 1)
    return -col, diag_inverse + mine


def solution(mesh):
    return jax.shard_map(
        local,
        mesh=mesh,
        in_specs=(P("prow", "pcol"), P("prow", None), P("prow", "pcol"), P()),
        out_specs=(P(("prow", "pcol"), None), P("prow", "pcol")),
        check_vma=False,
    )
```

time: 487 us -> 75.5 us (0.16)
  waiting for transfers between devices: 423 us -> 0 us
  Pallas kernels: 0 us -> 71.6 us
  matrix products: 35.8 us -> 0 us
  between operations: 13.8 us -> 0.67 us
  local copies, waits for them, and re-layouts: 6.18 us -> 0.01 us
    psum x2 -> x0, waiting for transfers between devices: 365 us -> none  [the longest x1 256 us: local(): total = lax.psum(correction, ('prow', 'pcol'))]
    pallas_call x0 -> x1, Pallas kernels: none -> 71.6 us  [local(): pl.pallas_call(kernel, out_shape=(jax.ShapeDtypeStruct((SH, W), F32), jax...]
    unnamed x4 -> x0, waiting for transfers between devices: 57.6 us -> none
    dot_general x2 -> x0, matrix products: 35.8 us -> none  [the longest x1 33.8 us: local(): jnp.dot(inverse_tiles, column_factor, precision=lax.Precision.HIGHEST, pr...]
    unnamed x5 -> x2, local copies, waits for them, and re-layouts: 6.1 us -> 0.01 us
  transfers between devices with their start and end apart: 3 -> 0, of which waited for: 3 -> 0; matrix products, arithmetic and copies ran while one was open for 0% -> 0% of each run, Pallas kernels for 0% -> 0%
where the time goes in v2:
time: 75.5 us; the launch traced here: 75.3 us
  Pallas kernels  71.6 us (95%)
  other arithmetic  3.02 us (4%)
    pallas_call x1, Pallas kernels, local(): pl.pallas_call(kernel, out_shape=(jax.ShapeDtypeStruct((SH, W), F32), jax...  71.6 us
    neg x1, other arithmetic, local(): return (-col, diag_inverse + mine)  1.62 us

profile of v2, /device:TPU:1, one launch (start us, length us, event | category | flops | bytes accessed | tf_op | source)
XLA Modules:
  0.0 75.3 jit_solution(9633310184825211721)
XLA Ops:
  0.6 0.0 copy-start
  0.7 71.6 %selected_inversion.1 = (f32[96,512]{1,0:T(8,128)}, f32[32,128]{1,0:T(8,128)}) custom-call(s32[192]{0:T(256)} %pat.1, f32[16,96,1536]{2,1,0:T(8,128)} %bitcast.1, f32[1536,512]{1,0:T(8,128)} %f_hbm.1), custom_call_target="tpu_custom_call" | custom-call | tf_op jit(solution)/shard_map/selected_inversion/pallas_call | solution.py:406
  72.2 0.0 copy-done
  72.2 1.4 %dynamic-slice_add_fusion = f32[32,32]{1,0:T(8,128)} fusion(f32[32,32]{1,0:T(8,128)S(1)} %copy-done, f32[32,128]{1,0:T(8,128)} %get-tuple-element.5, s32[]{:T(128)S(6)} %select_n.11), kind=kLoop, calls=%fused_computation | loop fusion | flops 1024 | bytes 12292 | tf_op jit(solution)/shard_map/add | solution.py:442
  73.6 1.6 %neg.3 = f32[96,512]{1,0:T(8,128)} negate(f32[96,512]{1,0:T(8,128)} %get-tuple-element.4) | non-fusion elementwise | flops 49152 | bytes 393216 | tf_op jit(solution)/shard_map/neg | solution.py:442
Async XLA Ops:
  0.6 71.6 %copy-start = (f32[32,32]{1,0:T(8,128)S(1)}, f32[32,32]{1,0:T(8,128)}, u32[]{:S(2)}) copy-start(f32[32,32]{1,0:T(8,128)} %param.6) | copy-start | bytes 12292

commit v3 on v2

--- a/solution.py
+++ b/solution.py
@@ -52,12 +52,12 @@
 ):
     r = lax.axis_index("prow")
     c = lax.axis_index("pcol")
-    x, y = r // NY, r % NY
-    z, core = c // NC, c % NC
+    x, y = r >> 2, r & (NY - 1)
+    z, core = c >> 1, c & (NC - 1)
     is_root = r == c
 
     def share_of(s):
-        h, zz = s // NZ, s % NZ
+        h, zz = s >> 3, s & (NZ - 1)
         dest_core = jnp.where(h == 0, 1 - core, core)
         return NC * zz + dest_core
 
@@ -88,22 +88,22 @@
     barrier = pltpu.get_barrier_semaphore()
     for dx, dy in XYORDER:
         pl.semaphore_signal(
-            barrier, inc=1, device_id=((x + dx) % NX * NY + (y + dy) % NY, c), device_id_type=MESH)
+            barrier, inc=1, device_id=(((x + dx) & (NX - 1)) * NY + ((y + dy) & (NY - 1)), c), device_id_type=MESH)
 
     @pl.loop(1, NP)
     def _(k):
-        pl.semaphore_signal(barrier, inc=1, device_id=(r, (c + k) % NP), device_id_type=MESH)
-
-    root_x, root_y = c // NY, c % NY
-    pos = (x - root_x + NX) % NX * NY + (y - root_y + NY) % NY
+        pl.semaphore_signal(barrier, inc=1, device_id=(r, (c + k) & (NP - 1)), device_id_type=MESH)
+
+    root_x, root_y = c >> 2, c & (NY - 1)
+    pos = ((x - root_x + NX) & (NX - 1)) * NY + ((y - root_y + NY) & (NY - 1))
     depth = [sum(((DEPTH[t][k] >> pos) & 1) << k for k in range(3)) for t in range(4)]
     sends = [[(SEND[t][d] >> pos) & 1 for d in range(4)] for t in range(4)]
     rank = [sum((((depth[u] < depth[t]) | ((depth[u] == depth[t]) & (u < t))).astype(jnp.int32) for u in range(4) if u != t), 0) for t in range(4)]
     order = [sum(t * (rank[t] == k).astype(jnp.int32) for t in range(4)) for k in range(4)]
-    peers = [((x + dx) % NX * NY + (y + dy) % NY, c) for dx, dy in DIRS]
+    peers = [(((x + dx) & (NX - 1)) * NY + ((y + dy) & (NY - 1)), c) for dx, dy in DIRS]
 
     def piece(t, s):
-        return fc.at[s // NSUB, pl.ds(pl.multiple_of(t * QR + (s % NSUB) * SR, 8), SR)]
+        return fc.at[s >> 1, pl.ds(pl.multiple_of(t * QR + (s & (NSUB - 1)) * SR, 8), SR)]
 
     def tree_copy(t, s, d):
         return pltpu.make_async_remote_copy(
@@ -116,15 +116,22 @@
             def _():
                 tree_copy(t, s, d).start()
 
+    def root_send():
+        for j in range(NCH):
+            root_load(j).wait()
+
+            @pl.loop(j * NSUB, (j + 1) * NSUB)
+            def _(s):
+                for t in range(4):
+                    tree_send(t, s)
+
     def relay(n):
         for t in range(4):
-            s = jnp.where(is_root, n, n - HOP * (depth[t] - 1))
-
-            @pl.when((s >= 0) & (s < NS))
+            s = n - HOP * (depth[t] - 1)
+
+            @pl.when(jnp.logical_not(is_root) & (s >= 0) & (s < NS))
             def _():
-                @pl.when(jnp.logical_not(is_root))
-                def _():
-                    pltpu.make_async_copy(piece(t, s), piece(t, s), t_r.at[t, s]).wait()
+                pltpu.make_async_copy(piece(t, s), piece(t, s), t_r.at[t, s]).wait()
                 tree_send(t, s)
 
     def tree_sent():
@@ -154,7 +161,7 @@
             masks = []
             for q in range(12):
                 row = r * TILE + SH * (NC * (4 * g + q // 3) + core) + 32 * (q % 3)
-                masks.append(pat[row // BLK].astype(F32))
+                masks.append(pat[row >> 7].astype(F32))
             for cb in range(W // 128):
                 v = fown[pl.ds(4 * g, 4), :, pl.ds(cb * 128, 128)].reshape(4 * SH, 128)
                 for b in range(3):
@@ -205,9 +212,9 @@
         away, off, first, count = ZCOPIES[slot]
         rows = pl.ds(first, count)
         return pltpu.make_async_remote_copy(
-            src_ref=pb.at[j, 1, (z + off + NZ) % NZ, rows], dst_ref=zb.at[j, slot, rows],
+            src_ref=pb.at[j, 1, (z + off + NZ) & (NZ - 1), rows], dst_ref=zb.at[j, slot, rows],
             send_sem=z_s.at[j], recv_sem=z_r.at[j, slot // 4],
-            device_id=(r, (c + NC * away + NP) % NP), device_id_type=MESH)
+            device_id=(r, (c + NC * away + NP) & (NP - 1)), device_id_type=MESH)
 
     def z_send(j, slot):
         z_copy(j, slot).start()
@@ -223,7 +230,7 @@
     def z_add(j):
         for slot in range(4):
             _, _, first, count = ZCOPIES[slot]
-            share, rows = (z + (NZ - 2 if slot < 2 else 2)) % NZ, pl.ds(first, count)
+            share, rows = (z + (NZ - 2 if slot < 2 else 2)) & (NZ - 1), pl.ds(first, count)
             pb[j, 1, share, rows] = pb[j, 1, share, rows] + zb[j, slot, rows]
 
     def z_first(j):
@@ -241,7 +248,7 @@
         total = pb[j, 1, z] + ((zb[j, 4] + zb[j, 5]) + (zb[j, 6] + zb[j, 7]))
         for q in range(3):
             row = r * TILE + SH * c + 32 * q
-            col_ref[pl.ds(32 * q, 32), cols(j)] = total[32 * q:32 * q + 32] * pat[row // BLK].astype(F32)
+            col_ref[pl.ds(32 * q, 32), cols(j)] = total[32 * q:32 * q + 32] * pat[row >> 7].astype(F32)
 
     def diag_product(j):
         for g in range(2):
@@ -258,7 +265,7 @@
 
     def d_send(g):
         for k, (dx, dy) in enumerate(XYORDER, 1):
-            to = (x + dx) % NX * NY + (y + dy) % NY
+            to = ((x + dx) & (NX - 1)) * NY + ((y + dy) & (NY - 1))
             pltpu.make_async_remote_copy(
                 src_ref=dp.at[to, :, d_cols(g)], dst_ref=db.at[k - 1, :, d_cols(g)],
                 send_sem=d_s.at[g], recv_sem=d_r.at[g],
@@ -292,14 +299,14 @@
         for i, j in enumerate(GROUPS[g]):
             e_send(j)
 
-            @pl.when(c // 4 == j)
+            @pl.when((c >> 2) == j)
             def _():
                 dz[c] = total[:, i * WC:(i + 1) * WC]
 
     def e_sent(j):
         pltpu.make_async_copy(dz.at[pl.ds(0, 3)], dz.at[pl.ds(0, 3)], e_s.at[j]).wait()
 
-        @pl.when(c // 4 != j)
+        @pl.when((c >> 2) != j)
         def _():
             pltpu.make_async_copy(dz.at[0], dz.at[0], e_s.at[j]).wait()
 
@@ -323,14 +330,14 @@
         add_exchanged(j)
         z_first(j)
 
-    a_wait(0, PRE)
-    split_a(0, PRE)
+    def split_first():
+        a_wait(0, PRE)
+        split_a(0, PRE)
+
+    pl.when(jnp.logical_not(is_root))(split_first)
     pl.semaphore_wait(barrier, NR - 1 + NP - 1)
-
-    @pl.when(is_root)
-    def _():
-        for j in range(NCH):
-            root_load(j).wait()
+    pl.when(is_root)(root_send)
+    pl.when(is_root)(split_first)
 
     @pl.loop(0, 10)
     def _(n):
@@ -378,11 +385,11 @@
     diag_product(3)
     d_send(1)
     z_second(2)
-    z_second(3)
     tree_sent()
     d_finish(0)
+    d_finish(1)
+    z_second(3)
     z_finish(0)
-    d_finish(1)
     z_finish(1)
     z_finish(2)
     for j in range(NCH):

time: 75.5 us -> 79.6 us (1.054)
  Pallas kernels: 71.6 us -> 75.7 us
    pallas_call x1, Pallas kernels: 71.6 us -> 75.7 us  [local(): pl.pallas_call(kernel, out_shape=(jax.ShapeDtypeStruct((SH, W), F32), jax...]
where the time goes in v3:
time: 79.6 us; the launch traced here: 79.4 us
  Pallas kernels  75.7 us (95%)
  other arithmetic  3.02 us (4%)
    pallas_call x1, Pallas kernels, local(): pl.pallas_call(kernel, out_shape=(jax.ShapeDtypeStruct((SH, W), F32), jax...  75.7 us
    neg x1, other arithmetic, local(): return (-col, diag_inverse + mine)  1.62 us

profile of v3, /device:TPU:1, one launch (start us, length us, event | category | flops | bytes accessed | tf_op | source)
XLA Modules:
  0.0 79.4 jit_solution(15036979261029879830)
XLA Ops:
  0.6 0.0 copy-start
  0.7 75.7 %selected_inversion.1 = (f32[96,512]{1,0:T(8,128)}, f32[32,128]{1,0:T(8,128)}) custom-call(s32[192]{0:T(256)} %pat.1, f32[16,96,1536]{2,1,0:T(8,128)} %bitcast.1, f32[1536,512]{1,0:T(8,128)} %f_hbm.1), custom_call_target="tpu_custom_call" | custom-call | tf_op jit(solution)/shard_map/selected_inversion/pallas_call | solution.py:413
  76.3 0.0 copy-done
  76.4 1.4 %dynamic-slice_add_fusion = f32[32,32]{1,0:T(8,128)} fusion(f32[32,32]{1,0:T(8,128)S(1)} %copy-done, f32[32,128]{1,0:T(8,128)} %get-tuple-element.5, s32[]{:T(128)S(6)} %select_n.11), kind=kLoop, calls=%fused_computation | loop fusion | flops 1024 | bytes 12292 | tf_op jit(solution)/shard_map/add | solution.py:449
  77.8 1.6 %neg.3 = f32[96,512]{1,0:T(8,128)} negate(f32[96,512]{1,0:T(8,128)} %get-tuple-element.4) | non-fusion elementwise | flops 49152 | bytes 393216 | tf_op jit(solution)/shard_map/neg | solution.py:449
Async XLA Ops:
  0.6 75.7 %copy-start = (f32[32,32]{1,0:T(8,128)S(1)}, f32[32,32]{1,0:T(8,128)}, u32[]{:S(2)}) copy-start(f32[32,32]{1,0:T(8,128)} %param.6) | copy-start | bytes 12292

commit v4 on v3

--- a/solution.py
+++ b/solution.py
@@ -116,22 +116,15 @@
             def _():
                 tree_copy(t, s, d).start()
 
-    def root_send():
-        for j in range(NCH):
-            root_load(j).wait()
-
-            @pl.loop(j * NSUB, (j + 1) * NSUB)
-            def _(s):
-                for t in range(4):
-                    tree_send(t, s)
-
     def relay(n):
         for t in range(4):
-            s = n - HOP * (depth[t] - 1)
-
-            @pl.when(jnp.logical_not(is_root) & (s >= 0) & (s < NS))
+            s = jnp.where(is_root, n, n - HOP * (depth[t] - 1))
+
+            @pl.when((s >= 0) & (s < NS))
             def _():
-                pltpu.make_async_copy(piece(t, s), piece(t, s), t_r.at[t, s]).wait()
+                @pl.when(jnp.logical_not(is_root))
+                def _():
+                    pltpu.make_async_copy(piece(t, s), piece(t, s), t_r.at[t, s]).wait()
                 tree_send(t, s)
 
     def tree_sent():
@@ -330,14 +323,14 @@
         add_exchanged(j)
         z_first(j)
 
-    def split_first():
-        a_wait(0, PRE)
-        split_a(0, PRE)
-
-    pl.when(jnp.logical_not(is_root))(split_first)
+    a_wait(0, PRE)
+    split_a(0, PRE)
     pl.semaphore_wait(barrier, NR - 1 + NP - 1)
-    pl.when(is_root)(root_send)
-    pl.when(is_root)(split_first)
+
+    @pl.when(is_root)
+    def _():
+        for j in range(NCH):
+            root_load(j).wait()
 
     @pl.loop(0, 10)
     def _(n):
@@ -385,11 +378,11 @@
     diag_product(3)
     d_send(1)
     z_second(2)
+    z_second(3)
     tree_sent()
     d_finish(0)
+    z_finish(0)
     d_finish(1)
-    z_second(3)
-    z_finish(0)
     z_finish(1)
     z_finish(2)
     for j in range(NCH):

time: 79.6 us -> 75.4 us (0.947)
  Pallas kernels: 75.7 us -> 71.4 us
    pallas_call x1, Pallas kernels: 75.7 us -> 71.4 us  [local(): pl.pallas_call(kernel, out_shape=(jax.ShapeDtypeStruct((SH, W), F32), jax...]
where the time goes in v4:
time: 75.4 us; the launch traced here: 75.1 us
  Pallas kernels  71.4 us (95%)
  other arithmetic  3.02 us (4%)
    pallas_call x1, Pallas kernels, local(): pl.pallas_call(kernel, out_shape=(jax.ShapeDtypeStruct((SH, W), F32), jax...  71.4 us
    neg x1, other arithmetic, local(): return (-col, diag_inverse + mine)  1.62 us

profile of v4, /device:TPU:1, one launch (start us, length us, event | category | flops | bytes accessed | tf_op | source)
XLA Modules:
  0.0 75.1 jit_solution(3108974094899557396)
XLA Ops:
  0.6 0.0 copy-start
  0.7 71.4 %selected_inversion.1 = (f32[96,512]{1,0:T(8,128)}, f32[32,128]{1,0:T(8,128)}) custom-call(s32[192]{0:T(256)} %pat.1, f32[16,96,1536]{2,1,0:T(8,128)} %bitcast.1, f32[1536,512]{1,0:T(8,128)} %f_hbm.1), custom_call_target="tpu_custom_call" | custom-call | tf_op jit(solution)/shard_map/selected_inversion/pallas_call | solution.py:406
  72.1 0.0 copy-done
  72.1 1.4 %dynamic-slice_add_fusion = f32[32,32]{1,0:T(8,128)} fusion(f32[32,32]{1,0:T(8,128)S(1)} %copy-done, f32[32,128]{1,0:T(8,128)} %get-tuple-element.5, s32[]{:T(128)S(6)} %select_n.11), kind=kLoop, calls=%fused_computation | loop fusion | flops 1024 | bytes 12292 | tf_op jit(solution)/shard_map/add | solution.py:442
  73.5 1.6 %neg.3 = f32[96,512]{1,0:T(8,128)} negate(f32[96,512]{1,0:T(8,128)} %get-tuple-element.4) | non-fusion elementwise | flops 49152 | bytes 393216 | tf_op jit(solution)/shard_map/neg | solution.py:442
Async XLA Ops:
  0.6 71.5 %copy-start = (f32[32,32]{1,0:T(8,128)S(1)}, f32[32,32]{1,0:T(8,128)}, u32[]{:S(2)}) copy-start(f32[32,32]{1,0:T(8,128)} %param.6) | copy-start | bytes 12292

commit v5 on v2

--- a/solution.py
+++ b/solution.py
@@ -400,8 +400,16 @@
     d_ref[...] = total
 
 
+def closing(col_ref, d_ref, diag_ref, column_ref, diagonal_ref):
+    place = lax.axis_index("pcol") & 3
+    mine = d_ref[:, 0:DR]
+    for k in range(1, WC // DR):
+        mine = jnp.where(place == k, d_ref[:, k * DR:(k + 1) * DR], mine)
+    column_ref[...] = -col_ref[...]
+    diagonal_ref[...] = diag_ref[...] + mine
+
+
 def local(inverse_tiles, factor_rows, diag_inverse, pattern):
-    c = lax.axis_index("pcol")
     dma = pltpu.SemaphoreType.DMA
     col, d = pl.pallas_call(
         kernel,
@@ -438,8 +446,14 @@
         compiler_params=pltpu.CompilerParams(collective_id=1, has_side_effects=True, vmem_limit_bytes=60 << 20),
         name="selected_inversion",
     )(pattern, inverse_tiles.reshape(NP, SH, TILE), factor_rows)
-    mine = lax.dynamic_slice_in_dim(d, (c % 4) * DR, DR, 1)
-    return -col, diag_inverse + mine
+    vmem = pl.BlockSpec(memory_space=pltpu.VMEM)
+    return pl.pallas_call(
+        closing,
+        out_shape=(jax.ShapeDtypeStruct((SH, W), F32), jax.ShapeDtypeStruct((DR, DR), F32)),
+        in_specs=[vmem] * 3,
+        out_specs=(vmem, vmem),
+        name="closing",
+    )(col, d, diag_inverse)
 
 
 def solution(mesh):

time: 75.5 us -> 74 us (0.980)
  other arithmetic: 3.02 us -> 0 us
  Pallas kernels: 71.6 us -> 73.3 us
    pallas_call x0 -> x1, Pallas kernels: none -> 1.84 us  [local(): pl.pallas_call(closing, out_shape=(jax.ShapeDtypeStruct((SH, W), F32), ja...]
    neg x1 -> x0, other arithmetic: 1.62 us -> none  [local(): return (-col, diag_inverse + mine)]
    add x1 -> x0, other arithmetic: 1.4 us -> none  [local(): return (-col, diag_inverse + mine)]
where the time goes in v5:
time: 74 us; the launch traced here: 73.9 us
  Pallas kernels  73.3 us (99%)
    pallas_call x1, Pallas kernels, local(): pl.pallas_call(kernel, out_shape=(jax.ShapeDtypeStruct((SH, W), F32), jax...  71.4 us
    pallas_call x1, Pallas kernels, local(): pl.pallas_call(closing, out_shape=(jax.ShapeDtypeStruct((SH, W), F32), ja...  1.84 us

profile of v5, /device:TPU:1, one launch (start us, length us, event | category | flops | bytes accessed | tf_op | source)
XLA Modules:
  0.0 73.9 jit_solution(16126629473610774296)
XLA Ops:
  0.6 71.4 %selected_inversion.1 = (f32[96,512]{1,0:T(8,128)}, f32[32,128]{1,0:T(8,128)}) custom-call(s32[192]{0:T(256)} %pat.1, f32[16,96,1536]{2,1,0:T(8,128)} %bitcast.1, f32[1536,512]{1,0:T(8,128)} %f_hbm.1), custom_call_target="tpu_custom_call" | custom-call | tf_op jit(solution)/shard_map/selected_inversion/pallas_call | solution.py:414
  72.1 1.8 %closing.1 = (f32[96,512]{1,0:T(8,128)}, f32[32,32]{1,0:T(8,128)}) custom-call(f32[96,512]{1,0:T(8,128)} %get-tuple-element.4.col_ref, f32[32,128]{1,0:T(8,128)} %get-tuple-element.5.d_ref, f32[32,32]{1,0:T(8,128)} %diag_ref.1), custom_call_target="tpu_custom_call" | custom-call | tf_op jit(solution)/shard_map/closing/pallas_call | solution.py:450
